TPU v7x, 128 devices: a whole 4x4x4 slice. The times are simulated.
128 devices in a mesh: ctx: 16 (over y, z_lo, core), kv: 8 (over x, z_hi).
Axes of the slice: x: 4, y: 4, z: 4 (z_hi: 2, z_lo: 2; z = z_hi * 2 + z_lo), core: 2. Of those that a mesh axis runs over, the one named last changes fastest.
Arguments:
- prompt_in: bfloat16 [256, 8192], P(None, 'ctx'), may hold values from -6 to 6
- step_in: bfloat16 [3, 64, 8192], P(None, None, 'ctx'), may hold values from -6 to 6
- norm_gain: bfloat16 [8192], P('ctx'), may hold values from 0.099609375 to 1.8984375
- query_weight: bfloat16 [8192, 8192], P('ctx', 'kv'), may hold values from -0.125 to 0.125
- key_weight: bfloat16 [8192, 1024], P('ctx', 'kv'), may hold values from -0.125 to 0.125
- value_weight: bfloat16 [8192, 1024], P('ctx', 'kv'), may hold values from -0.0625 to 0.0625
- out_weight: bfloat16 [8192, 8192], P('kv', 'ctx'), may hold values from -0.125 to 0.125
- key_cache: bfloat16 [8, 131072, 128], P('kv', 'ctx'), may hold values from -540 to 540
- value_cache: bfloat16 [8, 131072, 128], P('kv', 'ctx'), may hold values from -5 to 5
- cache_lengths: int32 [16], P('ctx'), may hold values from 2048 to 8192
- visible: int32 [64], replicated, may hold values from 1 to 256, as said below
Outputs:
- prompt_out: bfloat16 [256, 8192], P('kv', 'ctx')
- step_out: bfloat16 [3, 64, 8192], P(None, 'kv', 'ctx')
Inputs may be any that keep to these rules, and one draw needn't show every extreme that they name: `visible`: prompt tokens seen by each decode row.
All inputs are finite; a program needn't handle non-finite values.
Results may differ from a plain program's by a relative error of at most 0.035.
Values may be sent and summed in bfloat16 or wider, within the bound.
A program may use at most 192 MiB of HBM per device.

v0:
```python
import jax
import jax.numpy as jnp
from jax import lax
from jax.sharding import PartitionSpec as P

D = 8192
HD = 128
EPSILON = 1e-05


def normalize_rows(inputs, norm_gain):
    widened = inputs.astype(jnp.float32)
    scaled = (widened * norm_gain.astype(jnp.float32)).astype(jnp.bfloat16)
    squares = jnp.sum(widened * widened, axis=-1)
    return (scaled, squares)


def shard_attention(queries, key_shard, value_shard, length, extra_pairs, extra_mask):
    flat_rows, head_size = queries.shape
    block_rows = 512
    blocks = flat_rows // block_rows
    extra_count = extra_pairs.shape[0]
    slots_live = lax.broadcasted_iota(jnp.int32, (1, key_shard.shape[0]), 1) < length
    extra_keys = extra_pairs[:, :head_size]
    extra_values = extra_pairs[:, head_size:]
    factor = head_size ** (-0.5)

    def one_block(operands):
        query_block, mask_block = operands
        cache_scores = (
            jnp.einsum("fd,cd->fc", query_block, key_shard, preferred_element_type=jnp.float32)
            * factor
        )
        extra_scores = (
            jnp.einsum("fd,ed->fe", query_block, extra_keys, preferred_element_type=jnp.float32)
            * factor
        )
        cache_scores = jnp.where(slots_live, cache_scores, -jnp.inf)
        extra_scores = jnp.where(mask_block, extra_scores, -jnp.inf)
        highest = jnp.maximum(jnp.max(cache_scores, axis=1), jnp.max(extra_scores, axis=1))
        cache_weights = jnp.exp(cache_scores - highest[:, None]).astype(jnp.bfloat16)
        extra_weights = jnp.exp(extra_scores - highest[:, None]).astype(jnp.bfloat16)
        totals = jnp.sum(cache_weights, axis=1, dtype=jnp.float32) + jnp.sum(
            extra_weights, axis=1, dtype=jnp.float32
        )
        mixture = jnp.dot(cache_weights, value_shard, preferred_element_type=jnp.float32)
        mixture = mixture + jnp.dot(extra_weights, extra_values, preferred_element_type=jnp.float32)
        return (highest, totals, mixture)

    highest, totals, mixture = lax.map(
        one_block,
        (
            queries.reshape(blocks, block_rows, head_size),
            extra_mask.reshape(blocks, block_rows, extra_count),
        ),
    )
    return (
        highest.reshape(flat_rows),
        totals.reshape(flat_rows),
        mixture.reshape(flat_rows, head_size),
    )


def run_section(
    inputs,
    limits,
    owner_rows,
    owner_steps,
    store_fn,
    stores,
    norm_gain,
    query_weight,
    pair_weight,
    out_weight,
    key_shard,
    value_shard,
    length,
):
    step_sets, row_count, _ = inputs.shape
    device_place = lax.axis_index("ctx")
    owned_rows = row_count // lax.axis_size("ctx")
    scaled, squares = normalize_rows(inputs, norm_gain)
    query_part = jnp.einsum("srd,de->sre", scaled, query_weight, preferred_element_type=jnp.float32)
    pair_part = jnp.einsum("srd,de->rse", scaled, pair_weight, preferred_element_type=jnp.float32)
    query_sum, square_sum = lax.psum((query_part, squares), "ctx")
    pair_sum = lax.psum_scatter(
        pair_part.astype(jnp.bfloat16), "ctx", scatter_dimension=0, tiled=True
    ).astype(jnp.float32)
    inverse = lax.rsqrt(square_sum / D + EPSILON)
    queries = (query_sum * inverse[:, :, None]).astype(jnp.bfloat16)
    own_inverse = jnp.swapaxes(
        lax.dynamic_slice_in_dim(inverse, device_place * owned_rows, owned_rows, 1), 0, 1
    )
    pair_rows = (pair_sum * own_inverse[:, :, None]).astype(jnp.bfloat16)
    prompt_pairs, own_pairs = store_fn(pair_rows, stores)
    extra_pairs = jnp.concatenate(
        [prompt_pairs, own_pairs.reshape(-1, own_pairs.shape[-1])], axis=0
    )
    prompt_own = prompt_pairs.shape[0]
    rows_own = own_pairs.shape[0]
    step_total = own_pairs.shape[1]
    prompt_index = device_place * prompt_own + lax.broadcasted_iota(
        jnp.int32, (1, 1, prompt_own), 2
    )
    seen_prompt = prompt_index < limits[:, :, None]
    slot_ids = lax.broadcasted_iota(jnp.int32, (1, 1, rows_own * step_total), 2)
    slot_row = device_place * rows_own + slot_ids // step_total
    slot_step = slot_ids % step_total
    seen_own = (slot_row == owner_rows[:, :, None]) & (slot_step <= owner_steps[:, :, None])
    seen_keys = jnp.concatenate([seen_prompt, seen_own], axis=2)
    heads_per = queries.shape[2] // HD
    extra_count = seen_keys.shape[2]
    extra_mask = jnp.broadcast_to(
        seen_keys[:, :, None, :], (step_sets, row_count, heads_per, extra_count)
    )
    extra_mask = extra_mask.reshape(step_sets * row_count * heads_per, extra_count)
    flat_queries = queries.reshape(step_sets * row_count * heads_per, HD)
    highest, totals, mixture = shard_attention(
        flat_queries, key_shard, value_shard, length, extra_pairs, extra_mask
    )
    overall = lax.pmax(highest, "ctx")
    rescale = jnp.exp(highest - overall)
    totals, mixture = (
        lax.psum((totals * rescale).astype(jnp.bfloat16), "ctx").astype(jnp.float32),
        lax.psum((mixture * rescale[:, None]).astype(jnp.bfloat16), "ctx").astype(jnp.float32),
    )
    attended = (mixture / totals[:, None]).astype(jnp.bfloat16)
    attended = attended.reshape(step_sets, row_count, heads_per * HD)
    my_share = lax.psum_scatter(
        jnp.einsum("srk,kd->rsd", attended, out_weight, preferred_element_type=jnp.float32).astype(
            jnp.bfloat16
        ),
        "kv",
        scatter_dimension=0,
        tiled=True,
    ).astype(jnp.float32)
    return (jnp.swapaxes(my_share, 0, 1).astype(jnp.bfloat16), (prompt_pairs, own_pairs))


def on_device(
    prompt_in,
    step_in,
    norm_gain,
    query_weight,
    key_weight,
    value_weight,
    out_weight,
    key_cache,
    value_cache,
    cache_lengths,
    visible,
):
    ctx_count = lax.axis_size("ctx")
    prompt_total = prompt_in.shape[0]
    row_total = visible.shape[0]
    step_total = step_in.shape[0]
    prompt_own = prompt_total // ctx_count
    rows_own = row_total // ctx_count
    pair_weight = jnp.concatenate([key_weight, value_weight], axis=1)
    pair_width = pair_weight.shape[1]
    shared = (
        norm_gain,
        query_weight,
        pair_weight,
        out_weight,
        key_cache[0],
        value_cache[0],
        cache_lengths[0],
    )
    stores = (
        jnp.zeros((prompt_own, pair_width), jnp.bfloat16),
        jnp.zeros((rows_own, step_total, pair_width), jnp.bfloat16),
    )

    def keep_prompt(pair_rows, current):
        return (pair_rows[:, 0, :], current[1])

    prompt_limits = lax.broadcasted_iota(jnp.int32, (1, prompt_total), 1) + 1
    nobody = jnp.full((1, prompt_total), -1, jnp.int32)
    prompt_out, stores = run_section(
        prompt_in[None], prompt_limits, nobody, nobody, keep_prompt, stores, *shared
    )
    row_ids = lax.broadcasted_iota(jnp.int32, (1, row_total), 1)
    outputs = []
    for step_index in range(step_total):

        def keep_one(pair_rows, current, step_index=step_index):
            return (
                current[0],
                lax.dynamic_update_slice_in_dim(current[1], pair_rows, step_index, 1),
            )

        step_ids = jnp.full((1, row_total), step_index, jnp.int32)
        result, stores = run_section(
            step_in[step_index : step_index + 1],
            visible[None, :],
            row_ids,
            step_ids,
            keep_one,
            stores,
            *shared
        )
        outputs.append(result)
    step_out = jnp.concatenate(outputs, axis=0)
    return (prompt_out[0], step_out)


def solution(mesh):
    placed = (
        P(None, "ctx"),
        P(None, None, "ctx"),
        P("ctx"),
        P("ctx", "kv"),
        P("ctx", "kv"),
        P("ctx", "kv"),
        P("kv", "ctx"),
        P("kv", "ctx", None),
        P("kv", "ctx", None),
        P("ctx"),
        P(),
    )
    return jax.shard_map(
        on_device,
        mesh=mesh,
        in_specs=placed,
        out_specs=(P("kv", "ctx"), P(None, "kv", "ctx")),
        check_vma=False,
    )
```

profile of v0, /device:TPU:0, one launch (start us, length us, event | category | flops | bytes accessed | tf_op | source)
XLA Modules:
  0.0 1040.7 jit_solution(12494352496434197446)
XLA Ops:
  17.0 2.4 convolution_bitcast_fusion
  27.3 31.0 %all-reduce.6 = (f32[1,256]{1,0:T(1,128)S(1)}, f32[1,64]{1,0:T(1,128)S(1)}, f32[1,64]{1,0:T(1,128)S(1)}, f32[1,64]{1,0:T(1,128)S(1)}) all-reduce(f32[1,256]{1,0:T(1,128)S(1)} %bitcast.209, f32[1,64]{1,0:T(1,128)S(1)} %bitcast.213, f32[1,64]{1,0:T(1,128)S(1)} %bitcast.212, ...), channel_id=1, replica_groups=mesh['ctx'=16,'kv'=8] {'ctx'}, use_global_device_ids=true, to_apply=%region_2.0 | all-reduce | flops 448 | bytes 3584 | tf_op jit(solution)/shard_map/psum | solution.py:85
  63.9 63.7 %all-reduce.21.cloned.1.call-done = (bf16[64,1,256]{2,0,1:T(8,128)(2,1)}, bf16[64,1,256]{2,0,1:T(8,128)(2,1)}, bf16[64,1,256]{2,0,1:T(8,128)(2,1)}) async-done(((bf16[64,1,256]{2,0,1:T(8,128)(2,1)}, bf16[64,1,256]{2,0,1:T(8,128)(2,1)}, bf16[64,1,256]{2,0,1:T(8,128)(2,1)}), (bf16[64,1,256]{2,0,1:T(8,128)(2,1)}, bf16[64,1,256]{2,0,1:T(8,128)(2,1)}, ...) | async-done | bytes 98320
  129.9 115.8 %all-reduce.17.cloned.1.call-done = bf16[256,1,256]{2,1,0:T(2,128)(2,1)} async-done(((bf16[256,1,256]{2,1,0:T(2,128)(2,1)}), bf16[256,1,256]{2,1,0:T(2,128)(2,1)}) %all-reduce.17.cloned.1.call-update) | async-done | bytes 131088
  246.5 126.1 %all-reduce.19.cloned.1.call-done = (f32[1,256,1024]{2,1,0:T(8,128)}, f32[1,64,1024]{2,1,0:T(8,128)}, f32[1,64,1024]{2,1,0:T(8,128)}, f32[1,64,1024]{2,1,0:T(8,128)}) async-done(((f32[1,256,1024]{2,1,0:T(8,128)}, f32[1,64,1024]{2,1,0:T(8,128)}, f32[1,64,1024]{2,1,0:T(8,128)}, f32[1,64,1024]{2,1,0:T(8,128)}), (f32[1,256,1024]{2,1,0:T(8,128)}, f32[1,64,1024]{2,1,0:T(8,128)}, f32[1,64,1024]{2,1,0:T(8,128)}, ...) | async-done | bytes 1835024 | tf_op jit(solution)/shard_map/psum | solution.py:85
  374.2 110.1 %while.3 = (s32[]{:T(128)}, f32[4,512]{1,0:T(4,128)S(1)}, f32[4,512]{1,0:T(4,128)S(1)}, f32[4,512,128]{2,1,0:T(8,128)}, bf16[4,512,128]{2,1,0:T(8,128)(2,1)S(1)}...) while((s32[]{:T(128)}, f32[4,512]{1,0:T(4,128)S(1)}, ...), condition=%wide.region_9.10_spmd.clone, body=%wide.region_4.9_spmd.clone.sunk | while | flops 2192774144 | bytes 64227508 | solution.py:50
  375.0 8.6 fusion.144
  383.9 11.2 %convert_reduce_fusion.10 = (f32[512]{0:T(512)S(1)}, bf16[512,8192]{1,0:T(8,128)(2,1)}) fusion(f32[512]{0:T(512)S(1)} %max.55, f32[512,8192]{1,0:T(8,128)} %get-tuple-element.411, pred[8192]{0:T(1024)(128)(4,1)S(1)} %compare_reduce_fusion.2), kind=kLoop, calls=%fused_computation.1.clone.1 | loop fusion | flops 25165312 | bytes 25178112 | tf_op jit(solution)/shard_map/while/body/eval_jaxpr/reduce_sum | solution.py:43
  395.1 5.7 fusion.146
  402.5 8.6 fusion.144
  411.4 11.2 %convert_reduce_fusion.10 = (f32[512]{0:T(512)S(1)}, bf16[512,8192]{1,0:T(8,128)(2,1)}) fusion(f32[512]{0:T(512)S(1)} %max.55, f32[512,8192]{1,0:T(8,128)} %get-tuple-element.411, pred[8192]{0:T(1024)(128)(4,1)S(1)} %compare_reduce_fusion.2), kind=kLoop, calls=%fused_computation.1.clone.1 | loop fusion | flops 25165312 | bytes 25178112 | tf_op jit(solution)/shard_map/while/body/eval_jaxpr/reduce_sum | solution.py:43
  422.6 5.7 fusion.146
  430.0 8.6 fusion.144
  438.9 11.2 %convert_reduce_fusion.10 = (f32[512]{0:T(512)S(1)}, bf16[512,8192]{1,0:T(8,128)(2,1)}) fusion(f32[512]{0:T(512)S(1)} %max.55, f32[512,8192]{1,0:T(8,128)} %get-tuple-element.411, pred[8192]{0:T(1024)(128)(4,1)S(1)} %compare_reduce_fusion.2), kind=kLoop, calls=%fused_computation.1.clone.1 | loop fusion | flops 25165312 | bytes 25178112 | tf_op jit(solution)/shard_map/while/body/eval_jaxpr/reduce_sum | solution.py:43
  450.2 5.7 fusion.146
  457.6 8.6 fusion.144
  466.4 11.2 %convert_reduce_fusion.10 = (f32[512]{0:T(512)S(1)}, bf16[512,8192]{1,0:T(8,128)(2,1)}) fusion(f32[512]{0:T(512)S(1)} %max.55, f32[512,8192]{1,0:T(8,128)} %get-tuple-element.411, pred[8192]{0:T(1024)(128)(4,1)S(1)} %compare_reduce_fusion.2), kind=kLoop, calls=%fused_computation.1.clone.1 | loop fusion | flops 25165312 | bytes 25178112 | tf_op jit(solution)/shard_map/while/body/eval_jaxpr/reduce_sum | solution.py:43
  477.7 5.7 fusion.146
  485.6 9.7 fusion.88
  495.4 8.1 fusion.86
  503.8 19.0 %fusion.13 = (f32[512]{0:T(512)S(1)}, f32[512]{0:T(512)S(1)}, f32[512]{0:T(512)S(1)}, f32[512,8192]{1,0:T(8,128)}) fusion(pred[8192]{0:T(1024)(128)(4,1)S(1)} %iota_compare_fusion.1, f32[512,8192]{1,0:T(8,128)} %fusion.88, f32[512,8192]{1,0:T(8,128)} %fusion.86, bf16[512,128]{1,0:T(8,128)(2,1)S(1)} %squeeze.45, bf16[1,8192,128]{2,1,0:T(8,128)(2,1)S(1)} %bitcast.197), kind=kOutput, calls=%fused_computation.29 | convolution fusion | flops 1111489024 | bytes 52574208 | tf_op jit(solution)/shard_map/while/body/eval_jaxpr/fd,cd->fc/dot_general | solution.py:31
  523.2 55.9 %all-reduce.8 = (f32[2048]{0:T(1024)S(1)}, f32[512]{0:T(512)S(1)}, f32[512]{0:T(512)S(1)}, f32[512]{0:T(512)S(1)}) all-reduce(f32[2048]{0:T(1024)S(1)} %bitcast.201, f32[512]{0:T(512)S(1)} %max.51, f32[512]{0:T(512)S(1)} %max.50, f32[512]{0:T(512)S(1)} %max.49), channel_id=1, replica_groups=mesh['ctx'=16,'kv'=8] {'ctx'}, use_global_device_ids=true, to_apply=%region_10.11 | all-reduce | flops 3584 | bytes 28672 | tf_op jit(solution)/shard_map/pmax | solution.py:121
  579.1 25.1 %convert_reduce_fusion.4 = (f32[512]{0:T(512)S(1)}, bf16[512,8192]{1,0:T(8,128)(2,1)S(1)}, f32[512]{0:T(512)S(1)}, bf16[512,8192]{1,0:T(8,128)(2,1)}, f32[512]{0:T(512)S(1)}, /*index=5*/bf16[512,8192]{1,0:T(8,128)(2,1)}) fusion(f32[512]{0:T(512)S(1)} %max.49, f32[512,8192]{1,0:T(8,128)} %get-tuple-element.321, pred[8192]{0:T(1024)(128)(4,1)S(1)} %iota_compare_fusion.1, ...), kind=kLoop, calls=%fused_computation.26 | loop fusion | flops 75495936 | bytes 75517952 | tf_op jit(solution)/shard_map/while/body/eval_jaxpr/reduce_sum | solution.py:43
  604.3 5.7 fusion.80
  610.0 5.8 fusion.82
  618.3 2.4 fusion.33
  623.4 27.8 %all-reduce.9 = (bf16[2048]{0:T(1024)(128)(2,1)S(1)}, bf16[512]{0:T(512)(128)(2,1)S(1)}, bf16[512]{0:T(512)(128)(2,1)S(1)}, bf16[512]{0:T(512)(128)(2,1)S(1)}) all-reduce(bf16[2048]{0:T(1024)(128)(2,1)S(1)} %get-tuple-element.297, bf16[512]{0:T(512)(128)(2,1)S(1)} %get-tuple-element.293, ...), channel_id=1, replica_groups=mesh['ctx'=16,'kv'=8] {'ctx'}, use_global_device_ids=true, to_apply=%region_12.13 | all-reduce | flops 3584 | bytes 14336 | tf_op jit(solution)/shard_map/psum | solution.py:124
  651.3 90.8 %all-reduce.23.cloned.1.call-done = (bf16[2048,128]{1,0:T(8,128)(2,1)}, bf16[512,128]{1,0:T(8,128)(2,1)}, bf16[512,128]{1,0:T(8,128)(2,1)}, bf16[512,128]{1,0:T(8,128)(2,1)}) async-done(((bf16[2048,128]{1,0:T(8,128)(2,1)}, bf16[512,128]{1,0:T(8,128)(2,1)}, bf16[512,128]{1,0:T(8,128)(2,1)}, bf16[512,128]{1,0:T(8,128)(2,1)}), (bf16[2048,128]{1,0:T(8,128)(2,1)}, bf16[512,128]{1,0:T(8,128)(2,1)}, ...) | async-done | bytes 917520 | tf_op jit(solution)/shard_map/psum | solution.py:125
  751.1 65.1 %reduce-scatter.14.cloned.1.call-done = bf16[8,1,512]{2,0,1:T(8,128)(2,1)} async-done(((bf16[64,1,512]{2,0,1:T(8,128)(2,1)}), bf16[8,1,512]{2,0,1:T(8,128)(2,1)}) %reduce-scatter.14.cloned.1.call-update) | async-done | bytes 8208 | tf_op jit(solution)/shard_map/reduce_scatter | solution.py:129
  816.2 72.2 %reduce-scatter.12.cloned.1.call-done = bf16[8,1,512]{2,0,1:T(8,128)(2,1)} async-done(((bf16[64,1,512]{2,0,1:T(8,128)(2,1)}), bf16[8,1,512]{2,0,1:T(8,128)(2,1)}) %reduce-scatter.12.cloned.1.call-update) | async-done | bytes 8208 | tf_op jit(solution)/shard_map/reduce_scatter | solution.py:129
  888.4 72.3 %reduce-scatter.10.cloned.1.call-done = bf16[8,1,512]{2,0,1:T(8,128)(2,1)} async-done(((bf16[64,1,512]{2,0,1:T(8,128)(2,1)}), bf16[8,1,512]{2,0,1:T(8,128)(2,1)}) %reduce-scatter.10.cloned.1.call-update) | async-done | bytes 8208 | tf_op jit(solution)/shard_map/reduce_scatter | solution.py:129
  962.0 71.9 %reduce-scatter.8.cloned.1.call-done = bf16[32,1,512]{2,0,1:T(8,128)(2,1)} async-done(((bf16[256,1,512]{2,0,1:T(8,128)(2,1)}), bf16[32,1,512]{2,0,1:T(8,128)(2,1)}) %reduce-scatter.8.cloned.1.call-update) | async-done | bytes 32784 | tf_op jit(solution)/shard_map/reduce_scatter | solution.py:129
  (171 shorter events, 51.6 us)
Async XLA Ops:
  7.2 9.8 copy-start
  7.2 120.4 %all-reduce.21.cloned.1.call-start = ((), (), s32[]{:S(2)}) async-start(), calls=%async_computation.10 | async-start | bytes 196608
  14.7 231.0 %all-reduce.17.cloned.1.call-start = ((), (), s32[]{:S(2)}) async-start(), calls=%async_computation.8 | async-start | bytes 524288
  16.9 355.7 %all-reduce.19.cloned.1.call-start = ((), (), s32[]{:S(2)}) async-start(), calls=%async_computation.9 | async-start | bytes 3670016 | tf_op jit(solution)/shard_map/psum | solution.py:85
  25.0 717.0 %all-reduce.23.cloned.1.call-start = ((), (), s32[]{:S(2)}) async-start(), calls=%async_computation.11 | async-start | bytes 1835008 | tf_op jit(solution)/shard_map/psum | solution.py:125
  374.2 110.1 %copy-start.5 = (f32[1,64,1024]{2,1,0:T(8,128)S(1)}, f32[1,64,1024]{2,1,0:T(8,128)}, u32[]{:S(2)}) copy-start(f32[1,64,1024]{2,1,0:T(8,128)} %get-tuple-element.265) | copy-start | bytes 786436
  383.6 11.5 %copy-start.6 = (bf16[8192,128]{1,0:T(8,128)(2,1)S(1)}, bf16[8192,128]{1,0:T(8,128)(2,1)}, u32[]{:S(2)}) copy-start(bf16[8192,128]{1,0:T(8,128)(2,1)} %get-tuple-element.449) | copy-start | bytes 6291460 | tf_op jit(solution)/shard_map/while
  411.1 11.5 %copy-start.6 = (bf16[8192,128]{1,0:T(8,128)(2,1)S(1)}, bf16[8192,128]{1,0:T(8,128)(2,1)}, u32[]{:S(2)}) copy-start(bf16[8192,128]{1,0:T(8,128)(2,1)} %get-tuple-element.449) | copy-start | bytes 6291460 | tf_op jit(solution)/shard_map/while
  438.6 11.5 %copy-start.6 = (bf16[8192,128]{1,0:T(8,128)(2,1)S(1)}, bf16[8192,128]{1,0:T(8,128)(2,1)}, u32[]{:S(2)}) copy-start(bf16[8192,128]{1,0:T(8,128)(2,1)} %get-tuple-element.449) | copy-start | bytes 6291460 | tf_op jit(solution)/shard_map/while
  466.1 11.5 %copy-start.6 = (bf16[8192,128]{1,0:T(8,128)(2,1)S(1)}, bf16[8192,128]{1,0:T(8,128)(2,1)}, u32[]{:S(2)}) copy-start(bf16[8192,128]{1,0:T(8,128)(2,1)} %get-tuple-element.449) | copy-start | bytes 6291460 | tf_op jit(solution)/shard_map/while
  484.3 11.1 %copy-start.2 = (bf16[8192,128]{1,0:T(8,128)(2,1)S(1)}, bf16[8192,128]{1,0:T(8,128)(2,1)}, u32[]{:S(2)}) copy-start(bf16[8192,128]{1,0:T(8,128)(2,1)} %get-tuple-element.481) | copy-start | bytes 6291460
  485.6 17.8 %copy-start.4 = (f32[1,64,1024]{2,1,0:T(8,128)S(1)}, f32[1,64,1024]{2,1,0:T(8,128)}, u32[]{:S(2)}) copy-start(f32[1,64,1024]{2,1,0:T(8,128)} %get-tuple-element.266) | copy-start | bytes 786436
  579.1 25.1 %copy-start.7 = (bf16[8192,128]{1,0:T(8,128)(2,1)S(1)}, bf16[8192,128]{1,0:T(8,128)(2,1)}, u32[]{:S(2)}) copy-start(bf16[8192,128]{1,0:T(8,128)(2,1)} %get-tuple-element.524) | copy-start | bytes 6291460
  610.0 134.8 %copy-start.3 = (bf16[1024,512]{1,0:T(8,128)(2,1)S(1)}, bf16[1024,512]{1,0:T(8,128)(2,1)}, u32[]{:S(2)}) copy-start(bf16[1024,512]{1,0:T(8,128)(2,1)} %param.19) | copy-start | bytes 3145732
  610.0 423.9 %copy-start.1 = (bf16[512,1024]{1,0:T(8,128)(2,1)S(1)}, bf16[512,1024]{1,0:T(8,128)(2,1)}, u32[]{:S(2)}) copy-start(bf16[512,1024]{1,0:T(8,128)(2,1)} %param.16) | copy-start | bytes 3145732
  623.4 192.8 %reduce-scatter.14.cloned.1.call-start = ((), (), s32[]{:S(2)}) async-start(), calls=%async_computation.7 | async-start | bytes 73728 | tf_op jit(solution)/shard_map/reduce_scatter | solution.py:129
  745.7 142.7 %reduce-scatter.12.cloned.1.call-start = ((), (), s32[]{:S(2)}) async-start(), calls=%async_computation.6 | async-start | bytes 73728 | tf_op jit(solution)/shard_map/reduce_scatter | solution.py:129
  748.9 211.7 %reduce-scatter.10.cloned.1.call-start = ((), (), s32[]{:S(2)}) async-start(), calls=%async_computation.5 | async-start | bytes 73728 | tf_op jit(solution)/shard_map/reduce_scatter | solution.py:129
  749.9 283.9 %reduce-scatter.8.cloned.1.call-start = ((), (), s32[]{:S(2)}) async-start(), calls=%async_computation.4 | async-start | bytes 294912 | tf_op jit(solution)/shard_map/reduce_scatter | solution.py:129
Sparse Core Ops, SparseCore 0:
  14.9 112.6 all-reduce.20
  130.2 115.4 all-reduce.16
  248.5 124.1 all-reduce.18
  623.5 118.4 all-reduce.22
  745.8 70.3 reduce-scatter.13
  819.6 68.7 reduce-scatter.11
  891.9 68.6 reduce-scatter.9
  964.8 69.0 reduce-scatter.7
where the time goes:
time: 1040 us
  waiting for transfers between devices  678 us (65%)
  matrix products  133 us (13%)
  blocking collectives  115 us (11%)
  other arithmetic  90.4 us (9%)
  between operations  16.3 us (2%)
    reduce_scatter x4, waiting for transfers between devices, run_section(): lax.psum_scatter(jnp.einsum('srk,kd->rsd', attended, out_weight, preferre...  281 us
    unnamed x10, waiting for transfers between devices  180 us
    psum x1, waiting for transfers between devices, run_section(): query_sum, square_sum = lax.psum((query_part, squares), 'ctx')  126 us
    psum x1, waiting for transfers between devices, run_section(): lax.psum((mixture * rescale[:, None]).astype(jnp.bfloat16), 'ctx')  90.8 us
    dot_general x7, matrix products, one_block(): jnp.einsum('fd,cd->fc', query_block, key_shard, preferred_element_type=jn...  71.2 us
    reduce_sum x5, other arithmetic, one_block(): jnp.sum(cache_weights, axis=1, dtype=jnp.float32)  69.8 us
    pmax x1, blocking collectives, run_section(): overall = lax.pmax(highest, 'ctx')  55.9 us
    dot_general x7, matrix products, one_block(): jnp.dot(cache_weights, value_shard, preferred_element_type=jnp.float32)  36.7 us
  transfers between devices with their start and end apart: 8, of which 8 were waited for; matrix products, arithmetic and copies ran while one was open for 2% of the time, Pallas kernels for 0%

commit v1 on v0

--- a/solution.py
+++ b/solution.py
@@ -120,9 +120,13 @@
     )
     overall = lax.pmax(highest, "ctx")
     rescale = jnp.exp(highest - overall)
+
+    def _cover_column(s0):
+        return jax.lax.all_gather(s0, "ctx").sum(axis=0)
+
     totals, mixture = (
         lax.psum((totals * rescale).astype(jnp.bfloat16), "ctx").astype(jnp.float32),
-        lax.psum((mixture * rescale[:, None]).astype(jnp.bfloat16), "ctx").astype(jnp.float32),
+        _cover_column((mixture * rescale[:, None]).astype(jnp.bfloat16)).astype(jnp.float32),
     )
     attended = (mixture / totals[:, None]).astype(jnp.bfloat16)
     attended = attended.reshape(step_sets, row_count, heads_per * HD)

time: 1040 us -> 1010 us (0.971)
  matrix products: 133 us -> 104 us
  blocking collectives: 115 us -> 141 us
  other arithmetic: 90.4 us -> 72.2 us
  waiting for transfers between devices: 678 us -> 665 us
    psum x1 -> x0, waiting for transfers between devices: 90.8 us -> none  [run_section(): lax.psum((mixture * rescale[:, None]).astype(jnp.bfloat16), 'ctx')]
    all_gather x0 -> x4, waiting for transfers between devices: none -> 75 us  [_cover_column(): return jax.lax.all_gather(s0, 'ctx').sum(axis=0)]
    psum x1, blocking collectives: 27.8 us -> 54.2 us  [run_section(): lax.psum((totals * rescale).astype(jnp.bfloat16), 'ctx').astype(jnp.float32)]
    dot_general x7, matrix products: 71.2 us -> 47.3 us  [one_block(): jnp.einsum('fd,cd->fc', query_block, key_shard, preferred_element_type=jn...]
    reduce_sum x5, other arithmetic: 69.8 us -> 46.2 us  [one_block(): jnp.sum(cache_weights, axis=1, dtype=jnp.float32)]
    dot_general x7, matrix products: 36.7 us -> 24.9 us  [one_block(): jnp.dot(cache_weights, value_shard, preferred_element_type=jnp.float32)]
    reduce_sum x0 -> x4, other arithmetic: none -> 10.5 us  [_cover_column(): return jax.lax.all_gather(s0, 'ctx').sum(axis=0)]
    unnamed x10 -> x13, waiting for transfers between devices: 180 us -> 179 us
  transfers between devices with their start and end apart: 8 -> 11, of which waited for: 8 -> 9; matrix products, arithmetic and copies ran while one was open for 2% -> 6% of each run, Pallas kernels for 0% -> 0%
where the time goes in v1:
time: 1010 us
  waiting for transfers between devices  665 us (66%)
  blocking collectives  141 us (14%)
  matrix products  104 us (10%)
  other arithmetic  72.2 us (7%)
  between operations  16.4 us (2%)
    reduce_scatter x4, waiting for transfers between devices, run_section(): lax.psum_scatter(jnp.einsum('srk,kd->rsd', attended, out_weight, preferre...  284 us
    unnamed x13, waiting for transfers between devices  179 us
    psum x1, waiting for transfers between devices, run_section(): query_sum, square_sum = lax.psum((query_part, squares), 'ctx')  126 us
    all_gather x4, waiting for transfers between devices, _cover_column(): return jax.lax.all_gather(s0, 'ctx').sum(axis=0)  75 us
    pmax x1, blocking collectives, run_section(): overall = lax.pmax(highest, 'ctx')  56.1 us
    psum x1, blocking collectives, run_section(): lax.psum((totals * rescale).astype(jnp.bfloat16), 'ctx').astype(jnp.float32)  54.2 us
    dot_general x7, matrix products, one_block(): jnp.einsum('fd,cd->fc', query_block, key_shard, preferred_element_type=jn...  47.3 us
    reduce_sum x5, other arithmetic, one_block(): jnp.sum(cache_weights, axis=1, dtype=jnp.float32)  46.2 us
  transfers between devices with their start and end apart: 11, of which 9 were waited for; matrix products, arithmetic and copies ran while one was open for 6% of the time, Pallas kernels for 0%

profile of v1, /device:TPU:0, one launch (start us, length us, event | category | flops | bytes accessed | tf_op | source)
XLA Modules:
  0.0 1008.8 jit_solution(3724497780582293028)
XLA Ops:
  17.1 2.4 convolution_bitcast_fusion
  27.4 31.1 %all-reduce.6 = (f32[1,256]{1,0:T(1,128)S(1)}, f32[1,64]{1,0:T(1,128)S(1)}, f32[1,64]{1,0:T(1,128)S(1)}, f32[1,64]{1,0:T(1,128)S(1)}) all-reduce(f32[1,256]{1,0:T(1,128)S(1)} %bitcast.238, f32[1,64]{1,0:T(1,128)S(1)} %bitcast.242, f32[1,64]{1,0:T(1,128)S(1)} %bitcast.241, ...), channel_id=1, replica_groups=mesh['ctx'=16,'kv'=8] {'ctx'}, use_global_device_ids=true, to_apply=%region_2.0 | all-reduce | flops 448 | bytes 3584 | tf_op jit(solution)/shard_map/psum | solution.py:85
  64.4 63.3 %all-reduce.19.cloned.1.call-done = (bf16[64,1,256]{2,0,1:T(8,128)(2,1)}, bf16[64,1,256]{2,0,1:T(8,128)(2,1)}, bf16[64,1,256]{2,0,1:T(8,128)(2,1)}) async-done(((bf16[64,1,256]{2,0,1:T(8,128)(2,1)}, bf16[64,1,256]{2,0,1:T(8,128)(2,1)}, bf16[64,1,256]{2,0,1:T(8,128)(2,1)}), (bf16[64,1,256]{2,0,1:T(8,128)(2,1)}, bf16[64,1,256]{2,0,1:T(8,128)(2,1)}, ...) | async-done | bytes 98320
  130.0 115.8 %all-reduce.15.cloned.1.call-done = bf16[256,1,256]{2,1,0:T(2,128)(2,1)} async-done(((bf16[256,1,256]{2,1,0:T(2,128)(2,1)}), bf16[256,1,256]{2,1,0:T(2,128)(2,1)}) %all-reduce.15.cloned.1.call-update) | async-done | bytes 131088
  246.6 126.1 %all-reduce.17.cloned.1.call-done = (f32[1,256,1024]{2,1,0:T(8,128)}, f32[1,64,1024]{2,1,0:T(8,128)}, f32[1,64,1024]{2,1,0:T(8,128)}, f32[1,64,1024]{2,1,0:T(8,128)}) async-done(((f32[1,256,1024]{2,1,0:T(8,128)}, f32[1,64,1024]{2,1,0:T(8,128)}, f32[1,64,1024]{2,1,0:T(8,128)}, f32[1,64,1024]{2,1,0:T(8,128)}), (f32[1,256,1024]{2,1,0:T(8,128)}, f32[1,64,1024]{2,1,0:T(8,128)}, f32[1,64,1024]{2,1,0:T(8,128)}, ...) | async-done | bytes 1835024 | tf_op jit(solution)/shard_map/psum | solution.py:85
  373.9 9.7 fusion.94
  383.6 8.1 fusion.96
  395.5 18.9 %fusion.13 = (f32[512]{0:T(512)S(1)}, f32[512]{0:T(512)S(1)}, f32[512]{0:T(512)S(1)}, f32[512,8192]{1,0:T(8,128)}) fusion(pred[8192]{0:T(1024)(128)(4,1)S(1)} %iota_compare_fusion.1, f32[512,8192]{1,0:T(8,128)} %fusion.96, f32[512,8192]{1,0:T(8,128)} %fusion.94, bf16[512,128]{1,0:T(8,128)(2,1)S(1)} %squeeze.45, bf16[1,8192,128]{2,1,0:T(8,128)(2,1)S(1)} %copy-done.2), kind=kOutput, calls=%fused_computation.29 | convolution fusion | flops 1111489024 | bytes 52574208 | tf_op jit(solution)/shard_map/while/body/eval_jaxpr/fd,cd->fc/dot_general | solution.py:31
  414.7 25.3 %convert_reduce_fusion.4 = (f32[512]{0:T(512)S(1)}, bf16[512,8192]{1,0:T(8,128)(2,1)S(1)}, f32[512]{0:T(512)S(1)}, bf16[512,8192]{1,0:T(8,128)(2,1)}, f32[512]{0:T(512)S(1)}, /*index=5*/bf16[512,8192]{1,0:T(8,128)(2,1)}) fusion(f32[512]{0:T(512)S(1)} %max.49, f32[512,8192]{1,0:T(8,128)} %get-tuple-element.317, pred[8192]{0:T(1024)(128)(4,1)S(1)} %iota_compare_fusion.1, ...), kind=kLoop, calls=%fused_computation.26 | loop fusion | flops 75495936 | bytes 75517952 | tf_op jit(solution)/shard_map/while/body/eval_jaxpr/reduce_sum | solution.py:43
  440.1 3.0 fusion.92
  443.1 49.1 %while.3 = (s32[]{:T(128)}, f32[4,512]{1,0:T(4,128)S(1)}, f32[4,512]{1,0:T(4,128)S(1)}, f32[4,512,128]{2,1,0:T(8,128)}, bf16[4,512,128]{2,1,0:T(8,128)(2,1)S(1)}...) while((s32[]{:T(128)}, f32[4,512]{1,0:T(4,128)S(1)}, ...), condition=%wide.region_9.10_spmd.clone, body=%wide.region_4.9_spmd.clone.sunk | while | flops 2192774144 | bytes 64228008 | solution.py:50
  443.9 2.7 fusion.148
  446.7 5.2 convert_reduce_fusion.10
  456.1 2.7 fusion.148
  459.0 5.2 convert_reduce_fusion.10
  464.2 2.3 fusion.150
  468.4 2.7 fusion.148
  471.3 5.2 convert_reduce_fusion.10
  480.7 2.7 fusion.148
  483.6 5.2 convert_reduce_fusion.10
  492.2 56.1 %all-reduce.8 = (f32[2048]{0:T(1024)S(1)}, f32[512]{0:T(512)S(1)}, f32[512]{0:T(512)S(1)}, f32[512]{0:T(512)S(1)}) all-reduce(f32[2048]{0:T(1024)S(1)} %bitcast.230, f32[512]{0:T(512)S(1)} %max.51, f32[512]{0:T(512)S(1)} %max.50, f32[512]{0:T(512)S(1)} %max.49), channel_id=1, replica_groups=mesh['ctx'=16,'kv'=8] {'ctx'}, use_global_device_ids=true, to_apply=%region_10.11 | all-reduce | flops 3584 | bytes 28672 | tf_op jit(solution)/shard_map/pmax | solution.py:121
  550.3 6.3 fusion.90
  557.6 6.3 fusion.88
  566.6 54.2 %all-reduce.9 = (bf16[256,8]{1,0:T(8,128)(2,1)S(1)}, bf16[64,8]{1,0:T(8,128)(2,1)S(1)}, bf16[64,8]{1,0:T(8,128)(2,1)S(1)}, bf16[64,8]{1,0:T(8,128)(2,1)S(1)}) all-reduce(bf16[256,8]{1,0:T(8,128)(2,1)S(1)} %div.99, bf16[64,8]{1,0:T(8,128)(2,1)S(1)} %div.117, bf16[64,8]{1,0:T(8,128)(2,1)S(1)} %div.111, ...), channel_id=1, replica_groups=mesh['ctx'=16,'kv'=8] {'ctx'}, use_global_device_ids=true, to_apply=%region_12.13 | all-reduce | flops 3584 | bytes 14336 | tf_op jit(solution)/shard_map/psum | solution.py:128
  624.7 29.7 %all-gather.14.cloned.1.call-done = bf16[8192,128]{1,0:T(8,128)(2,1)} async-done(((bf16[512,128]{1,0:T(8,128)(2,1)}), bf16[8192,128]{1,0:T(8,128)(2,1)}) %all-gather.14.cloned.1.call-update) | async-done | bytes 2097168 | tf_op jit(solution)/shard_map/all_gather | solution.py:125
  663.4 45.3 %all-gather.8.cloned.1.call-done = bf16[16,2048,128]{2,1,0:T(8,128)(2,1)} async-done(((bf16[1,2048,128]{2,1,0:T(8,128)(2,1)}), bf16[16,2048,128]{2,1,0:T(8,128)(2,1)}) %all-gather.8.cloned.1.call-update) | async-done | bytes 8388624 | tf_op jit(solution)/shard_map/all_gather | solution.py:125
  708.7 4.8 reduce_sum.172
  714.0 2.4 fusion.19
  716.4 66.8 %reduce-scatter.10.cloned.1.call-done = bf16[8,1,512]{2,0,1:T(8,128)(2,1)} async-done(((bf16[64,1,512]{2,0,1:T(8,128)(2,1)}), bf16[8,1,512]{2,0,1:T(8,128)(2,1)}) %reduce-scatter.10.cloned.1.call-update) | async-done | bytes 8208 | tf_op jit(solution)/shard_map/reduce_scatter | solution.py:133
  783.2 72.8 %reduce-scatter.12.cloned.1.call-done = bf16[8,1,512]{2,0,1:T(8,128)(2,1)} async-done(((bf16[64,1,512]{2,0,1:T(8,128)(2,1)}), bf16[8,1,512]{2,0,1:T(8,128)(2,1)}) %reduce-scatter.12.cloned.1.call-update) | async-done | bytes 8208 | tf_op jit(solution)/shard_map/reduce_scatter | solution.py:133
  856.0 72.6 %reduce-scatter.14.cloned.1.call-done = bf16[8,1,512]{2,0,1:T(8,128)(2,1)} async-done(((bf16[64,1,512]{2,0,1:T(8,128)(2,1)}), bf16[8,1,512]{2,0,1:T(8,128)(2,1)}) %reduce-scatter.14.cloned.1.call-update) | async-done | bytes 8208 | tf_op jit(solution)/shard_map/reduce_scatter | solution.py:133
  929.9 72.4 %reduce-scatter.8.cloned.1.call-done = bf16[32,1,512]{2,0,1:T(8,128)(2,1)} async-done(((bf16[256,1,512]{2,0,1:T(8,128)(2,1)}), bf16[32,1,512]{2,0,1:T(8,128)(2,1)}) %reduce-scatter.8.cloned.1.call-update) | async-done | bytes 32784 | tf_op jit(solution)/shard_map/reduce_scatter | solution.py:133
  (182 shorter events, 65.3 us)
Async XLA Ops:
  7.2 10.0 copy-start
  7.2 120.5 %all-reduce.19.cloned.1.call-start = ((), (), s32[]{:S(2)}) async-start(), calls=%async_computation.14 | async-start | bytes 196608
  8.9 374.7 %copy-start.2 = (bf16[1,8192,128]{2,1,0:T(8,128)(2,1)S(1)}, bf16[1,8192,128]{2,1,0:T(8,128)(2,1)}, u32[]{:S(2)}) copy-start(bf16[1,8192,128]{2,1,0:T(8,128)(2,1)} %param.20) | copy-start | bytes 6291460
  14.9 230.9 %all-reduce.15.cloned.1.call-start = ((), (), s32[]{:S(2)}) async-start(), calls=%async_computation.12 | async-start | bytes 524288
  17.1 355.6 %all-reduce.17.cloned.1.call-start = ((), (), s32[]{:S(2)}) async-start(), calls=%async_computation.13 | async-start | bytes 3670016 | tf_op jit(solution)/shard_map/psum | solution.py:85
  25.1 595.7 %all-gather.10.cloned.1.call-start = ((), (), s32[]{:S(2)}) async-start(), calls=%async_computation.9 | async-start | bytes 2228224 | tf_op jit(solution)/shard_map/all_gather | solution.py:125
  373.9 17.8 %copy-start.4 = (f32[1,64,1024]{2,1,0:T(8,128)S(1)}, f32[1,64,1024]{2,1,0:T(8,128)}, u32[]{:S(2)}) copy-start(f32[1,64,1024]{2,1,0:T(8,128)} %get-tuple-element.266) | copy-start | bytes 786436
  414.7 25.3 %copy-start.5 = (bf16[1,8192,128]{2,1,0:T(8,128)(2,1)S(1)}, bf16[1,8192,128]{2,1,0:T(8,128)(2,1)}, u32[]{:S(2)}) copy-start(bf16[1,8192,128]{2,1,0:T(8,128)(2,1)} %param.21) | copy-start | bytes 6291460
  446.5 5.4 copy-start.6
  458.8 5.4 copy-start.6
  471.1 5.4 copy-start.6
  483.4 5.4 copy-start.6
  492.2 72.7 %copy-start.3 = (f32[4,512,128]{2,1,0:T(8,128)S(1)}, f32[4,512,128]{2,1,0:T(8,128)}, u32[]{:S(2)}) copy-start(f32[4,512,128]{2,1,0:T(8,128)} %get-tuple-element.138) | copy-start | bytes 3145732
  550.2 72.6 %all-gather.12.cloned.1.call-start = ((), (), s32[]{:S(2)}) async-start(), calls=%async_computation.10 | async-start | bytes 2228224 | tf_op jit(solution)/shard_map/all_gather | solution.py:125
  557.5 96.9 %all-gather.14.cloned.1.call-start = ((), (), s32[]{:S(2)}) async-start(), calls=%async_computation.11 | async-start | bytes 2228224 | tf_op jit(solution)/shard_map/all_gather | solution.py:125
  564.8 437.4 %copy-start.1 = (bf16[512,1024]{1,0:T(8,128)(2,1)S(1)}, bf16[512,1024]{1,0:T(8,128)(2,1)}, u32[]{:S(2)}) copy-start(bf16[512,1024]{1,0:T(8,128)(2,1)} %param.16) | copy-start | bytes 3145732
  564.8 143.8 %all-gather.8.cloned.1.call-start = ((), (), s32[]{:S(2)}) async-start(), calls=%async_computation.4 | async-start | bytes 8912896 | tf_op jit(solution)/shard_map/all_gather | solution.py:125
  566.1 217.1 %reduce-scatter.10.cloned.1.call-start = ((), (), s32[]{:S(2)}) async-start(), calls=%async_computation.6 | async-start | bytes 73728 | tf_op jit(solution)/shard_map/reduce_scatter | solution.py:133
  658.7 197.3 %reduce-scatter.12.cloned.1.call-start = ((), (), s32[]{:S(2)}) async-start(), calls=%async_computation.7 | async-start | bytes 73728 | tf_op jit(solution)/shard_map/reduce_scatter | solution.py:133
  661.0 267.5 %reduce-scatter.14.cloned.1.call-start = ((), (), s32[]{:S(2)}) async-start(), calls=%async_computation.8 | async-start | bytes 73728 | tf_op jit(solution)/shard_map/reduce_scatter | solution.py:133
  663.3 338.9 %reduce-scatter.8.cloned.1.call-start = ((), (), s32[]{:S(2)}) async-start(), calls=%async_computation.5 | async-start | bytes 294912 | tf_op jit(solution)/shard_map/reduce_scatter | solution.py:133
Sparse Core Ops, SparseCore 0:
  15.0 112.5 all-reduce.18
  130.3 115.4 all-reduce.14
  248.5 124.0 all-reduce.16
  550.3 32.6 all-gather.9
  584.7 34.3 all-gather.11
  620.8 33.6 all-gather.13
  656.2 52.3 all-gather.7
  712.6 70.5 reduce-scatter.9
  787.2 68.7 reduce-scatter.11
  859.8 68.7 reduce-scatter.13
  933.1 69.0 reduce-scatter.7
